TPU v7x, 32 devices: a whole 2x2x4 slice. The times are simulated.
32 devices in a mesh: grp: 2 (over y), ex: 8 (over z, x), ffn: 2 (over core).
Axes of the slice: x: 2, y: 2, z: 4, core: 2. Of those that a mesh axis runs over, the one named last changes fastest.
Arguments:
- tokens_in: bfloat16 [8192, 4096], P(('grp', 'ex'), 'ffn'), parts along dimension 0, may hold values from -6 to 6
- grad_out: bfloat16 [8192, 14336], P(('grp', 'ex'), 'ffn'), parts along dimension 0, may hold values from -6 to 6
- proj_in: bfloat16 [4096, 32], P('ffn'), may hold values from -0.09375 to 0.09375
- proj_out: bfloat16 [14336, 32], P('ffn'), may hold values from -0.046875 to 0.046875
- segment_ids: int32 [16, 512], P(('grp', 'ex')), parts along dimension 0, may hold values from 0 to 15, never falling along the last dimension, each value on 1 to 64 neighbouring positions
- query_grads: float32 [256, 1024], P(('grp', 'ex')), parts along dimension 0, may hold values from -3 to 3
Outputs:
- scores: float32 [256, 128], P(('grp', 'ex')), parts along dimension 0
There are 2 independent parts, one for each index of `grp`. A program takes and returns all parts, laid end to end along the dimension named above; an argument that names none is the same for every part. Nothing has to cross between parts.
Inputs may be any that keep to these rules, and one draw needn't show every extreme that they name: `segment_ids`: in each row the numbers never fall; each of the 16 examples of a row has 1 to 64 tokens, one exactly that many.
All inputs are finite; a program needn't handle non-finite values.
Results may differ from a plain program's by a relative error of at most 0.0003.
Values sent between devices are 32-bit elements; how exact they have to be, the bound alone decides.
A program may use at most 128 MiB of HBM per device.

v0:
```python
import jax
import jax.numpy as jnp
from jax import lax
from jax.sharding import PartitionSpec as P

EX_DEV = 16


def per_device(tokens_in, grad_out, proj_in, proj_out, segment_ids, query_grads):
    rank = proj_in.shape[1]
    width = rank * rank
    rows = tokens_in.shape[0]
    out_part = jnp.dot(grad_out, proj_out, preferred_element_type=jnp.float32)
    in_part = jnp.dot(tokens_in, proj_in, preferred_element_type=jnp.float32)
    out_side, in_side = lax.psum((out_part, in_part), "ffn")
    outer = (out_side[:, :, None] * in_side[:, None, :]).reshape(rows, width)
    labels = jnp.arange(EX_DEV, dtype=jnp.int32)
    member = (segment_ids[0][:, None] == labels[None, :]).astype(jnp.float32)
    counts = jnp.sum(member, axis=0)
    sums = lax.dot_general(member, outer, (((0,), (0,)), ((), ())), precision=lax.Precision.HIGHEST)
    example_grads = sums / counts[:, None]
    total = EX_DEV * lax.axis_size("ex")
    local_term = lax.dot_general(
        example_grads, example_grads, (((0,), (0,)), ((), ())), precision=lax.Precision.HIGHEST
    )
    fisher_raw = lax.psum(local_term, "ex") / total
    damping = 0.1 * jnp.trace(fisher_raw) / width
    fisher = fisher_raw + damping * jnp.eye(width, dtype=jnp.float32)
    chol = jnp.linalg.cholesky(fisher)
    scale = jnp.sqrt(jnp.float32(width))
    halfway = lax.linalg.triangular_solve(chol, query_grads.T, left_side=True, lower=True)
    precond = lax.linalg.triangular_solve(
        chol, halfway, left_side=True, lower=True, transpose_a=True
    )
    return (
        jnp.dot(
            example_grads,
            lax.all_gather(precond, "ex", axis=1, tiled=True),
            precision=lax.Precision.HIGHEST,
        )
        / scale
    )


def solution(mesh):
    in_specs = (
        P(("grp", "ex"), "ffn"),
        P(("grp", "ex"), "ffn"),
        P("ffn", None),
        P("ffn", None),
        P(("grp", "ex"), None),
        P(("grp", "ex"), None),
    )
    out_specs = P(("grp", "ex"), None)
    return jax.shard_map(
        per_device, mesh=mesh, in_specs=in_specs, out_specs=out_specs, check_vma=False
    )
```

profile of v0, /device:TPU:0, one launch (start us, length us, event | category | flops | bytes accessed | tf_op | source)
XLA Modules:
  0.0 604.4 jit_solution(15917842097387756758)
XLA Ops:
  10.4 6.0 fusion.96
  16.6 20.6 %all-reduce.7.cloned.1.call-done = (f32[512,32]{0,1:T(8,128)}, f32[512,32]{0,1:T(8,128)}) async-done(((f32[512,32]{0,1:T(8,128)}, f32[512,32]{0,1:T(8,128)}), (f32[512,32]{0,1:T(8,128)}, f32[512,32]{0,1:T(8,128)})) %all-reduce.7.cloned.1.call-update) | async-done | bytes 131088 | tf_op jit(solution)/shard_map/psum | solution.py:15
  39.5 5.0 fusion.98
  44.5 157.6 %all-reduce.5.cloned.1.call-done = f32[1024,1024]{0,1:T(8,128)} async-done(((f32[1024,1024]{0,1:T(8,128)}), f32[1024,1024]{0,1:T(8,128)}) %all-reduce.5.cloned.1.call-update) | async-done | bytes 4194320 | tf_op jit(solution)/shard_map/psum | solution.py:26
  202.2 2.9 select_reduce_fusion
  205.7 5.0 select_add_fusion
  210.8 5.5 copy.46
  216.2 4.5 fusion
  222.7 11.7 %cholesky.222 = f32[128,128]{1,0:T(8,128)S(1)} custom-call(f32[128,128]{1,0:T(8,128)S(1)} %cholesky.577), custom_call_target="Cholesky" | custom-call | tf_op jit(solution)/shard_map/jit(cholesky)/cholesky | solution.py:29
  235.1 9.8 %custom-call.64 = f32[1,128,128]{1,2,0:T(8,128)S(1)} custom-call(f32[1,128,128]{2,1,0:T(8,128)S(1)} %get-tuple-element.50), custom_call_target="InvertDiagBlocksLowerTriangular" | custom-call | tf_op jit(solution)/shard_map/jit(cholesky)/cholesky | solution.py:29
  248.3 11.7 %cholesky.243 = f32[128,128]{1,0:T(8,128)S(1)} custom-call(f32[128,128]{1,0:T(8,128)S(1)} %cholesky.581), custom_call_target="Cholesky" | custom-call | tf_op jit(solution)/shard_map/jit(cholesky)/cholesky | solution.py:29
  260.3 9.8 %custom-call.65 = f32[1,128,128]{1,2,0:T(8,128)S(1)} custom-call(f32[1,128,128]{2,1,0:T(8,128)S(1)} %get-tuple-element.48), custom_call_target="InvertDiagBlocksLowerTriangular" | custom-call | tf_op jit(solution)/shard_map/jit(cholesky)/cholesky | solution.py:29
  274.0 2.4 convolution_subtract_fusion.1
  276.5 11.7 %cholesky.466 = f32[128,128]{1,0:T(8,128)S(1)} custom-call(f32[128,128]{1,0:T(8,128)S(1)} %cholesky.586), custom_call_target="Cholesky" | custom-call | tf_op jit(solution)/shard_map/jit(cholesky)/cholesky | solution.py:29
  289.0 9.8 %custom-call.66 = f32[1,128,128]{1,2,0:T(8,128)S(1)} custom-call(f32[1,128,128]{2,1,0:T(8,128)S(1)} %get-tuple-element.46), custom_call_target="InvertDiagBlocksLowerTriangular" | custom-call | tf_op jit(solution)/shard_map/jit(cholesky)/cholesky | solution.py:29
  300.0 3.5 convolution_subtract_fusion.2
  303.6 11.7 %cholesky.485 = f32[128,128]{1,0:T(8,128)S(1)} custom-call(f32[128,128]{1,0:T(8,128)S(1)} %cholesky.591), custom_call_target="Cholesky" | custom-call | tf_op jit(solution)/shard_map/jit(cholesky)/cholesky | solution.py:29
  316.1 9.8 %custom-call.67 = f32[1,128,128]{1,2,0:T(8,128)S(1)} custom-call(f32[1,128,128]{2,1,0:T(8,128)S(1)} %get-tuple-element.44), custom_call_target="InvertDiagBlocksLowerTriangular" | custom-call | tf_op jit(solution)/shard_map/jit(cholesky)/cholesky | solution.py:29
  327.0 3.1 convolution_subtract_fusion.3
  330.2 11.9 %cholesky.504 = f32[128,128]{1,0:T(8,128)S(1)} custom-call(f32[128,128]{1,0:T(8,128)S(1)} %cholesky.596), custom_call_target="Cholesky" | custom-call | tf_op jit(solution)/shard_map/jit(cholesky)/cholesky | solution.py:29
  342.8 9.8 %custom-call.68 = f32[1,128,128]{1,2,0:T(8,128)S(1)} custom-call(f32[1,128,128]{2,1,0:T(8,128)S(1)} %get-tuple-element.42), custom_call_target="InvertDiagBlocksLowerTriangular" | custom-call | tf_op jit(solution)/shard_map/jit(cholesky)/cholesky | solution.py:29
  353.8 3.1 convolution_subtract_fusion.4
  356.9 11.7 %cholesky.524 = f32[128,128]{1,0:T(8,128)S(1)} custom-call(f32[128,128]{1,0:T(8,128)S(1)} %cholesky.601), custom_call_target="Cholesky" | custom-call | tf_op jit(solution)/shard_map/jit(cholesky)/cholesky | solution.py:29
  369.3 9.8 %custom-call.69 = f32[1,128,128]{1,2,0:T(8,128)S(1)} custom-call(f32[1,128,128]{2,1,0:T(8,128)S(1)} %get-tuple-element.40), custom_call_target="InvertDiagBlocksLowerTriangular" | custom-call | tf_op jit(solution)/shard_map/jit(cholesky)/cholesky | solution.py:29
  380.1 2.9 convolution_subtract_fusion.5
  383.0 11.7 %cholesky.544 = f32[128,128]{1,0:T(8,128)S(1)} custom-call(f32[128,128]{1,0:T(8,128)S(1)} %cholesky.606), custom_call_target="Cholesky" | custom-call | tf_op jit(solution)/shard_map/jit(cholesky)/cholesky | solution.py:29
  395.5 9.8 %custom-call.70 = f32[1,128,128]{1,2,0:T(8,128)S(1)} custom-call(f32[1,128,128]{2,1,0:T(8,128)S(1)} %get-tuple-element.38), custom_call_target="InvertDiagBlocksLowerTriangular" | custom-call | tf_op jit(solution)/shard_map/jit(cholesky)/cholesky | solution.py:29
  408.4 11.7 %cholesky.562 = f32[128,128]{1,0:T(8,128)S(1)} custom-call(f32[128,128]{1,0:T(8,128)S(1)} %convolution_subtract_fusion.6), custom_call_target="Cholesky" | custom-call | tf_op jit(solution)/shard_map/jit(cholesky)/cholesky | solution.py:29
  430.6 4.9 select_select_fusion
  435.4 28.5 %while.1 = (s32[]{:T(128)}, f32[1024,1024]{0,1:T(8,128)}, s32[8,2]{0,1:T(2,128)S(1)}, f32[8,128,128]{2,1,0:T(8,128)}, s32[]{:T(128)}) while((s32[]{:T(128)}, f32[1024,1024]{0,1:T(8,128)}, s32[8,2]{0,1:T(2,128)S(1)}, f32[8,128,128]{2,1,0:T(8,128)}, s32[]{:T(128)}) %tuple.51), condition=%wide.while_cond, body=%wide.while_body.sunk | while | flops 2 | bytes 393329 | solution.py:32
  463.9 79.6 %custom-call.71 = f32[8,128,128]{1,2,0:T(8,128)S(1)} custom-call(f32[8,128,128]{2,1,0:T(8,128)} %get-tuple-element.12), custom_call_target="InvertDiagBlocksLowerTriangular" | custom-call | tf_op jit(solution)/shard_map/triangular_solve | solution.py:32
  564.6 31.4 %all_gather.3 = f32[1024,128]{0,1:T(8,128)S(1)} all-gather(f32[1024,16]{0,1:T(8,128)S(1)} %constant_dynamic-update-slice_fusion.36), channel_id=1, replica_groups=mesh['grp'=2,'ex'=8,'ffn'=2] {'ex'}, dimensions={1}, use_global_device_ids=true | all-gather | bytes 589824 | tf_op jit(solution)/shard_map/all_gather | solution.py:38
  (163 shorter events, 83.6 us)
Async XLA Ops:
  6.5 1.6 copy-start
  6.5 30.7 %all-reduce.7.cloned.1.call-start = ((), (), s32[]{:S(2)}) async-start(), calls=%async_computation.1 | async-start | bytes 262144 | tf_op jit(solution)/shard_map/psum | solution.py:15
  10.4 6.1 %copy-start.4 = (s32[1,512]{1,0:T(1,128)S(1)}, s32[1,512]{1,0:T(1,128)}, u32[]{:S(2)}) copy-start(s32[1,512]{1,0:T(1,128)} %param.10) | copy-start | bytes 6148
  16.5 185.7 %all-reduce.5.cloned.1.call-start = ((), (), s32[]{:S(2)}) async-start(), calls=%async_computation | async-start | bytes 8388608 | tf_op jit(solution)/shard_map/psum | solution.py:26
  220.7 1.9 copy-start.2
  272.1 2.0 copy-start.1
  430.6 113.0 %copy-start.3 = (f32[16,1024]{1,0:T(8,128)S(1)}, f32[16,1024]{1,0:T(8,128)}, u32[]{:S(2)}) copy-start(f32[16,1024]{1,0:T(8,128)} %param.11) | copy-start | bytes 196612
Sparse Core Ops, SparseCore 0:
  16.6 20.6 all-reduce.6
  44.6 157.4 all-reduce.4
where the time goes:
time: 611 us; the launch traced here: 604 us
  other arithmetic  266 us (44%)
  waiting for transfers between devices  178 us (29%)
  matrix products  62.2 us (10%)
  local copies, waits for them, and re-layouts  46.7 us (8%)
  blocking collectives  31.4 us (5%)
  between operations  20 us (3%)
    another operation x30, other arithmetic, per_device(): chol = jnp.linalg.cholesky(fisher)  167 us
    psum x1, waiting for transfers between devices, per_device(): fisher_raw = lax.psum(local_term, 'ex') / total  158 us
    another operation x3, other arithmetic, per_device(): lax.linalg.triangular_solve(chol, halfway, left_side=True, lower=True, tr...  84.5 us
    all_gather x1, blocking collectives, per_device(): lax.all_gather(precond, 'ex', axis=1, tiled=True)  31.4 us
    another operation x40, local copies, waits for them, and re-layouts  28.4 us
    another operation x14, matrix products, per_device(): chol = jnp.linalg.cholesky(fisher)  26.1 us
    psum x1, waiting for transfers between devices, per_device(): out_side, in_side = lax.psum((out_part, in_part), 'ffn')  20.6 us
  transfers between devices with their start and end apart: 2, of which 2 were waited for; matrix products, arithmetic and copies ran while one was open for 0% of the time, Pallas kernels for 0%

commit v1 on v0

--- a/solution.py
+++ b/solution.py
@@ -4,9 +4,10 @@
 from jax.sharding import PartitionSpec as P
 
 EX_DEV = 16
+HIGH = lax.Precision.HIGHEST
 
 
-def per_device(tokens_in, grad_out, proj_in, proj_out, segment_ids, query_grads):
+def example_means(tokens_in, grad_out, proj_in, proj_out, segment_ids):
     rank = proj_in.shape[1]
     width = rank * rank
     rows = tokens_in.shape[0]
@@ -17,11 +18,16 @@
     labels = jnp.arange(EX_DEV, dtype=jnp.int32)
     member = (segment_ids[0][:, None] == labels[None, :]).astype(jnp.float32)
     counts = jnp.sum(member, axis=0)
-    sums = lax.dot_general(member, outer, (((0,), (0,)), ((), ())), precision=lax.Precision.HIGHEST)
-    example_grads = sums / counts[:, None]
+    sums = lax.dot_general(member, outer, (((0,), (0,)), ((), ())), precision=HIGH)
+    return sums / counts[:, None]
+
+
+def primal(tokens_in, grad_out, proj_in, proj_out, segment_ids, query_grads):
+    example_grads = example_means(tokens_in, grad_out, proj_in, proj_out, segment_ids)
+    width = example_grads.shape[1]
     total = EX_DEV * lax.axis_size("ex")
     local_term = lax.dot_general(
-        example_grads, example_grads, (((0,), (0,)), ((), ())), precision=lax.Precision.HIGHEST
+        example_grads, example_grads, (((0,), (0,)), ((), ())), precision=HIGH
     )
     fisher_raw = lax.psum(local_term, "ex") / total
     damping = 0.1 * jnp.trace(fisher_raw) / width
@@ -32,14 +38,29 @@
     precond = lax.linalg.triangular_solve(
         chol, halfway, left_side=True, lower=True, transpose_a=True
     )
-    return (
-        jnp.dot(
-            example_grads,
-            lax.all_gather(precond, "ex", axis=1, tiled=True),
-            precision=lax.Precision.HIGHEST,
-        )
-        / scale
+    gathered = lax.all_gather(precond, "ex", axis=1, tiled=True)
+    return jnp.dot(example_grads, gathered, precision=HIGH) / scale
+
+
+def dual(tokens_in, grad_out, proj_in, proj_out, segment_ids, query_grads):
+    example_grads = example_means(tokens_in, grad_out, proj_in, proj_out, segment_ids)
+    width = example_grads.shape[1]
+    total = EX_DEV * lax.axis_size("ex")
+    queries = lax.all_gather(query_grads, "ex", axis=0, tiled=True)
+    everyone = lax.all_gather(example_grads, "ex", axis=0, tiled=True)
+    gram = lax.dot_general(everyone, everyone, (((1,), (1,)), ((), ())), precision=HIGH) / total
+    damping = 0.1 * jnp.trace(gram) / width
+    gram = gram + damping * jnp.eye(total, dtype=jnp.float32)
+    cross = lax.dot_general(everyone, queries, (((1,), (1,)), ((), ())), precision=HIGH)
+    chol = jnp.linalg.cholesky(gram)
+    mine = lax.axis_index("ex") * EX_DEV + jnp.arange(EX_DEV)
+    pick = (jnp.arange(total)[:, None] == mine[None, :]).astype(jnp.float32)
+    halfway = lax.linalg.triangular_solve(chol, pick, left_side=True, lower=True)
+    rows = lax.linalg.triangular_solve(
+        chol, halfway, left_side=True, lower=True, transpose_a=True
     )
+    scores = lax.dot_general(rows, cross, (((0,), (0,)), ((), ())), precision=HIGH)
+    return scores / jnp.sqrt(jnp.float32(width))
 
 
 def solution(mesh):
@@ -52,6 +73,12 @@
         P(("grp", "ex"), None),
     )
     out_specs = P(("grp", "ex"), None)
+
+    def per_device(*args):
+        width = args[2].shape[1] ** 2
+        fewer = EX_DEV * mesh.shape["ex"] < width
+        return (dual if fewer else primal)(*args)
+
     return jax.shard_map(
         per_device, mesh=mesh, in_specs=in_specs, out_specs=out_specs, check_vma=False
     )

time: 611 us -> 117 us (0.19); the launches traced: 604 us -> 117 us
  other arithmetic: 266 us -> 24.1 us
  waiting for transfers between devices: 178 us -> 0.03 us
  matrix products: 62.2 us -> 12.3 us
  local copies, waits for them, and re-layouts: 46.7 us -> 1.79 us
  blocking collectives: 31.4 us -> 64.3 us
    another operation x33 -> x6, other arithmetic: 252 us -> 22.9 us  [the longest x4 12.4 us: dual(): chol = jnp.linalg.cholesky(gram)]
    psum x2 -> x1, waiting for transfers between devices: 178 us -> 0.01 us  [example_means(): out_side, in_side = lax.psum((out_part, in_part), 'ffn')]
    another operation x44 -> x2, matrix products: 46.7 us -> 0.4 us  [the longest x1 0.21 us: dual(): lax.linalg.triangular_solve(chol, pick, left_side=True, lower=True)]
    another operation x70 -> x1, local copies, waits for them, and re-layouts: 35.5 us -> 0.1 us  [dual(): chol = jnp.linalg.cholesky(gram)]
    all_gather x1 -> x2, blocking collectives: 31.4 us -> 64.3 us  [the longest x1 33 us: dual(): queries = lax.all_gather(query_grads, 'ex', axis=0, tiled=True)]
    dot_general x5 -> x6, matrix products: 15.5 us -> 11.9 us  [the longest x1 6.03 us: example_means(): out_part = jnp.dot(grad_out, proj_out, preferred_element_type=jnp.float32)]
  transfers between devices with their start and end apart: 2 -> 1, of which waited for: 2 -> 0; matrix products, arithmetic and copies ran while one was open for 0% -> 0% of each run, Pallas kernels for 0% -> 0%
where the time goes in v1:
time: 117 us
  blocking collectives  64.3 us (55%)
  other arithmetic  24.1 us (21%)
  between operations  14.1 us (12%)
  matrix products  12.3 us (11%)
  local copies, waits for them, and re-layouts  1.79 us (2%)
    all_gather x1, blocking collectives, dual(): queries = lax.all_gather(query_grads, 'ex', axis=0, tiled=True)  33 us
    all_gather x1, blocking collectives, dual(): everyone = lax.all_gather(example_grads, 'ex', axis=0, tiled=True)  31.3 us
    another operation x4, other arithmetic, dual(): chol = jnp.linalg.cholesky(gram)  12.4 us
    another operation x2, other arithmetic, dual(): lax.linalg.triangular_solve(chol, halfway, left_side=True, lower=True, tr...  10.5 us
    dot_general x1, matrix products, example_means(): out_part = jnp.dot(grad_out, proj_out, preferred_element_type=jnp.float32)  6.03 us
  transfers between devices with their start and end apart: 1, of which 0 were waited for; matrix products, arithmetic and copies ran while one was open for 0% of the time, Pallas kernels for 0%

profile of v1, /device:TPU:0, one launch (start us, length us, event | category | flops | bytes accessed | tf_op | source)
XLA Modules:
  0.0 116.7 jit_solution(18227209873142102831)
XLA Ops:
  6.5 0.0 copy-start
  6.5 0.0 copy-start.1
  6.5 0.0 all-reduce.3.cloned.1.call-start
  6.5 1.6 %copy-done = bf16[512,2048]{1,0:T(8,128)(2,1)S(1)} copy-done((bf16[512,2048]{1,0:T(8,128)(2,1)S(1)}, bf16[512,2048]{1,0:T(8,128)(2,1)}, u32[]{:S(2)}) %copy-start) | copy-done | bytes 2097176
  8.1 2.3 %fusion.10 = f32[512,32]{0,1:T(8,128)} fusion(bf16[512,2048]{1,0:T(8,128)(2,1)S(1)} %copy-done, bf16[2048,32]{0,1:T(8,128)(2,1)} %param.8), kind=kOutput, calls=%fused_computation.26 | convolution fusion | flops 67108864 | bytes 2293760 | tf_op jit(solution)/shard_map/dot_general | solution.py:15
  10.4 0.0 copy-done.1
  10.4 0.0 copy-start.2
  10.4 0.0 copy-start.3
  10.4 6.0 %fusion.9 = f32[512,32]{0,1:T(8,128)} fusion(bf16[512,7168]{1,0:T(8,128)(2,1)} %param.7, bf16[7168,32]{0,1:T(8,128)(2,1)S(1)} %copy-done.1), kind=kOutput, calls=%fused_computation.25 | convolution fusion | flops 234881024 | bytes 7864320 | tf_op jit(solution)/shard_map/dot_general | solution.py:14
  16.4 0.0 all-reduce.3.cloned.1.call-update
  16.5 0.0 copy-done.2
  16.5 33.0 %all_gather.7 = f32[128,1024]{1,0:T(8,128)S(1)} all-gather(f32[16,1024]{1,0:T(8,128)S(1)} %copy-done.2), channel_id=1, replica_groups=mesh['grp'=2,'ex'=8,'ffn'=2] {'ex'}, dimensions={0}, use_global_device_ids=true | all-gather | bytes 589824 | tf_op jit(solution)/shard_map/all_gather | solution.py:49
  49.5 0.1 copy.18
  49.6 0.0 copy-done.3
  49.6 0.1 convert_reduce_fusion
  49.7 0.0 all-reduce.3.cloned.1.call-done
  49.8 1.1 broadcast_multiply_fusion
  50.9 1.1 convolution_divide_fusion
  52.0 31.3 %all_gather.6 = f32[128,1024]{1,0:T(8,128)S(1)} all-gather(f32[16,1024]{1,0:T(8,128)S(1)} %convolution_divide_fusion), channel_id=1, replica_groups=mesh['grp'=2,'ex'=8,'ffn'=2] {'ex'}, dimensions={0}, use_global_device_ids=true | all-gather | bytes 589824 | tf_op jit(solution)/shard_map/all_gather | solution.py:50
  83.3 1.2 %select_reduce_fusion.1 = (f32[]{:T(128)}, f32[128,128]{0,1:T(8,128)S(1)}) fusion(pred[128,128]{0,1:T(32,128)(4,1)S(1)} %copy.18, f32[128,1024]{1,0:T(8,128)S(1)} %all_gather.6), kind=kOutput, calls=%fused_computation.16 | convolution fusion | flops 201375744 | bytes 606212 | tf_op jit(solution)/shard_map/dot_general | solution.py:51
  84.4 0.1 copy.20
  85.2 11.7 %cholesky.17 = f32[128,128]{1,0:T(8,128)S(1)} custom-call(f32[128,128]{1,0:T(8,128)S(1)} %fusion.6), custom_call_target="Cholesky" | custom-call | tf_op jit(solution)/shard_map/jit(cholesky)/cholesky | solution.py:55
  97.0 0.6 compare_reduce_fusion
  97.6 0.7 fusion
  98.3 9.8 %custom-call.8 = f32[1,128,128]{1,2,0:T(8,128)S(1)} custom-call(f32[1,128,128]{2,1,0:T(8,128)S(1)} %fusion), custom_call_target="InvertDiagBlocksLowerTriangular" | custom-call | tf_op jit(solution)/shard_map/triangular_solve | solution.py:59
  108.1 0.2 fusion.3
  108.3 0.2 fusion.1
  108.5 0.6 fusion.11
  109.1 0.8 convolution_multiply_fusion.1
  (4 shorter events, 0.1 us)
Async XLA Ops:
  6.5 1.6 %copy-start = (bf16[512,2048]{1,0:T(8,128)(2,1)S(1)}, bf16[512,2048]{1,0:T(8,128)(2,1)}, u32[]{:S(2)}) copy-start(bf16[512,2048]{1,0:T(8,128)(2,1)} %param.6) | copy-start | bytes 6291460
  6.5 3.9 %copy-start.1 = (bf16[7168,32]{0,1:T(8,128)(2,1)S(1)}, bf16[7168,32]{0,1:T(8,128)(2,1)}, u32[]{:S(2)}) copy-start(bf16[7168,32]{0,1:T(8,128)(2,1)} %param.9) | copy-start | bytes 1376260
  6.5 43.2 %all-reduce.3.cloned.1.call-start = ((), (), s32[]{:S(2)}) async-start(), calls=%async_computation | async-start | bytes 262144 | tf_op jit(solution)/shard_map/psum | solution.py:16
  10.4 6.1 %copy-start.2 = (f32[16,1024]{1,0:T(8,128)S(1)}, f32[16,1024]{1,0:T(8,128)}, u32[]{:S(2)}) copy-start(f32[16,1024]{1,0:T(8,128)} %param.11) | copy-start | bytes 196612
  10.4 39.2 %copy-start.3 = (s32[1,512]{1,0:T(1,128)S(1)}, s32[1,512]{1,0:T(1,128)}, u32[]{:S(2)}) copy-start(s32[1,512]{1,0:T(1,128)} %param.10) | copy-start | bytes 6148
Sparse Core Ops, SparseCore 0:
  16.6 20.6 all-reduce.2

commit v2 on v1

--- a/solution.py
+++ b/solution.py
@@ -1,6 +1,10 @@
+import functools
+
 import jax
 import jax.numpy as jnp
 from jax import lax
+from jax.experimental import pallas as pl
+from jax.experimental.pallas import tpu as pltpu
 from jax.sharding import PartitionSpec as P
 
 EX_DEV = 16
@@ -42,25 +46,198 @@
     return jnp.dot(example_grads, gathered, precision=HIGH) / scale
 
 
-def dual(tokens_in, grad_out, proj_in, proj_out, segment_ids, query_grads):
-    example_grads = example_means(tokens_in, grad_out, proj_in, proj_out, segment_ids)
-    width = example_grads.shape[1]
-    total = EX_DEV * lax.axis_size("ex")
-    queries = lax.all_gather(query_grads, "ex", axis=0, tiled=True)
-    everyone = lax.all_gather(example_grads, "ex", axis=0, tiled=True)
-    gram = lax.dot_general(everyone, everyone, (((1,), (1,)), ((), ())), precision=HIGH) / total
-    damping = 0.1 * jnp.trace(gram) / width
-    gram = gram + damping * jnp.eye(total, dtype=jnp.float32)
-    cross = lax.dot_general(everyone, queries, (((1,), (1,)), ((), ())), precision=HIGH)
-    chol = jnp.linalg.cholesky(gram)
-    mine = lax.axis_index("ex") * EX_DEV + jnp.arange(EX_DEV)
-    pick = (jnp.arange(total)[:, None] == mine[None, :]).astype(jnp.float32)
-    halfway = lax.linalg.triangular_solve(chol, pick, left_side=True, lower=True)
-    rows = lax.linalg.triangular_solve(
-        chol, halfway, left_side=True, lower=True, transpose_a=True
-    )
-    scores = lax.dot_general(rows, cross, (((0,), (0,)), ((), ())), precision=HIGH)
-    return scores / jnp.sqrt(jnp.float32(width))
+STEPS = 10
+CHUNK = 1024
+NT = (((1,), (1,)), ((), ()))
+
+
+def dot(a, b):
+    return jnp.dot(a, b, precision=HIGH, preferred_element_type=jnp.float32)
+
+
+def dot_nt(a, b):
+    return lax.dot_general(a, b, NT, precision=HIGH, preferred_element_type=jnp.float32)
+
+
+def kernel(
+    n, tok, grad, pin, pout, seg, qry, out,
+    tok_v, grad_v, pin_v, pout_v, seg_v, mine, theirs, e_all, q_all, part, part_in,
+    load_sem, chunk_sem, side_send, side_recv, e_send, e_recv, q_send, q_recv, p_send, p_recv,
+):
+    me, core = lax.axis_index("ex"), lax.axis_index("ffn")
+    rank = pin.shape[1]
+    half = rank // 2
+    width = rank * rank
+    cols = width // 2
+    total = n * EX_DEV
+    rows = pl.ds(pl.multiple_of(me * EX_DEV, EX_DEV), EX_DEV)
+
+    loads = [
+        pltpu.make_async_copy(
+            qry.at[:, pl.ds(pl.multiple_of(core * cols, cols), cols)], q_all.at[rows], load_sem.at[0]
+        ),
+        pltpu.make_async_copy(pin, pin_v, load_sem.at[1]),
+        pltpu.make_async_copy(tok, tok_v, load_sem.at[2]),
+        pltpu.make_async_copy(pout, pout_v, load_sem.at[3]),
+        pltpu.make_async_copy(seg, seg_v, load_sem.at[4]),
+    ]
+    chunks = [
+        pltpu.make_async_copy(
+            grad.at[:, pl.ds(k * CHUNK, CHUNK)], grad_v.at[:, pl.ds(k * CHUNK, CHUNK)], chunk_sem.at[k]
+        )
+        for k in range(grad.shape[1] // CHUNK)
+    ]
+    for copy in loads + chunks:
+        copy.start()
+
+    barrier = pltpu.get_barrier_semaphore()
+    peers = [lax.rem(me + k, n) for k in range(1, n)]
+    for peer in peers:
+        pl.semaphore_signal(barrier, inc=1, device_id={"ex": peer}, device_id_type=pl.DeviceIdType.MESH)
+    pl.semaphore_signal(barrier, inc=1, device_id={"ffn": 1 - core}, device_id_type=pl.DeviceIdType.MESH)
+    pl.semaphore_wait(barrier, n)
+
+    def spread(ref, send, recv):
+        copies = [
+            pltpu.make_async_remote_copy(
+                src_ref=ref.at[rows], dst_ref=ref.at[rows],
+                send_sem=send.at[k], recv_sem=recv.at[k],
+                device_id={"ex": peer}, device_id_type=pl.DeviceIdType.MESH,
+            )
+            for k, peer in enumerate(peers)
+        ]
+        for copy in copies:
+            copy.start()
+        return copies
+
+    def across(src, dst, send, recv):
+        copy = pltpu.make_async_remote_copy(
+            src_ref=src, dst_ref=dst, send_sem=send, recv_sem=recv,
+            device_id={"ffn": 1 - core}, device_id_type=pl.DeviceIdType.MESH,
+        )
+        copy.start()
+        return copy
+
+    loads[0].wait()
+    q_copies = spread(q_all, q_send, q_recv)
+
+    loads[1].wait()
+    loads[2].wait()
+    in_part = jnp.dot(tok_v[...], pin_v[...], preferred_element_type=jnp.float32)
+    mine[rank:, :] = in_part.T
+    in_copy = across(
+        mine.at[pl.ds(rank, rank)], theirs.at[pl.ds(half, rank)], side_send.at[0], side_recv.at[0]
+    )
+
+    loads[3].wait()
+    acc = jnp.zeros((grad.shape[0], rank), jnp.float32)
+    for k, copy in enumerate(chunks):
+        copy.wait()
+        span = slice(k * CHUNK, (k + 1) * CHUNK)
+        acc += jnp.dot(grad_v[:, span], pout_v[span, :], preferred_element_type=jnp.float32)
+    mine[:rank, :] = acc.T
+    keep = pl.ds(pl.multiple_of(core * half, half), half)
+    give = pl.ds(pl.multiple_of((1 - core) * half, half), half)
+    out_copy = across(mine.at[give], theirs.at[pl.ds(0, half)], side_send.at[1], side_recv.at[1])
+
+    loads[4].wait()
+    labels = lax.broadcasted_iota(jnp.int32, (EX_DEV, seg_v.shape[1]), 0)
+    member = (jnp.broadcast_to(seg_v[...], labels.shape) == labels).astype(jnp.float32)
+    counts = jnp.sum(member, axis=1, keepdims=True)
+
+    in_copy.wait()
+    in_side = mine[rank:, :] + theirs[half:, :]
+    in_tile = jnp.concatenate([in_side] * (128 // rank), axis=0)
+    out_copy.wait()
+    out_side = mine[keep, :] + theirs[:half, :]
+    masked = jnp.concatenate([member * out_side[i : i + 1, :] for i in range(half)], axis=0)
+    sums = dot_nt(masked, in_tile)
+    per = 128 // rank
+    place = lax.broadcasted_iota(jnp.int32, (EX_DEV, 128), 1) // rank
+    for g in range(cols // 128):
+        block = sums[g * per * EX_DEV : (g * per + 1) * EX_DEV]
+        for k in range(1, per):
+            row = (g * per + k) * EX_DEV
+            block = jnp.where(place == k, sums[row : row + EX_DEV], block)
+        e_all[rows, g * 128 : (g + 1) * 128] = block / counts
+    e_copies = spread(e_all, e_send, e_recv)
+    for copy in q_copies:
+        copy.wait()
+    for copy in e_copies:
+        copy.wait()
+
+    everyone = e_all[...]
+    part[:, :total] = dot_nt(everyone, everyone)
+    part[:, total:] = dot_nt(everyone, q_all[...])
+    p_copy = across(part, part_in, p_send, p_recv)
+    p_copy.wait()
+
+    whole = part[...] + part_in[...]
+    gram = whole[:, :total] * (1.0 / total)
+    cross = whole[:, total:]
+    r = lax.broadcasted_iota(jnp.int32, (total, total), 0)
+    c = lax.broadcasted_iota(jnp.int32, (total, total), 1)
+    eye = (r == c).astype(jnp.float32)
+    trace = jnp.sum(jnp.sum(gram * eye, axis=1, keepdims=True), axis=0, keepdims=True)
+    damping = (0.1 / width) * trace
+    gram = gram + damping * eye
+    bound = jnp.max(jnp.sum(jnp.abs(gram), axis=0, keepdims=True), axis=1, keepdims=True)
+    bound = jnp.minimum(bound, trace + damping) * 1.0001
+    low = damping / bound
+    y = gram / bound
+    x = eye / bound
+    for _ in range(STEPS):
+        scale = 4.0 / ((1.0 + low) * (1.0 + low))
+        factor = scale * ((1.0 + low) * eye - y)
+        both = dot(jnp.concatenate([y, x], axis=0), factor)
+        y, x = both[:total], both[total:]
+        low = jnp.minimum(scale * low, 1.0)
+    part_in[:, :total] = x
+    own = part_in[rows, :total]
+    r16 = lax.broadcasted_iota(jnp.int32, (EX_DEV, total), 0)
+    c16 = lax.broadcasted_iota(jnp.int32, (EX_DEV, total), 1)
+    left = (r16 + me * EX_DEV == c16).astype(jnp.float32) - dot(own, gram)
+    own = own + dot(left, x)
+    out[...] = dot(own, cross) * (1.0 / width ** 0.5)
+
+
+def dual(n, tokens_in, grad_out, proj_in, proj_out, segment_ids, query_grads):
+    tok, rank = tokens_in.shape[0], proj_in.shape[1]
+    cols = rank * rank // 2
+    total = n * EX_DEV
+    dma = pltpu.SemaphoreType.DMA
+    return pl.pallas_call(
+        functools.partial(kernel, n),
+        out_shape=jax.ShapeDtypeStruct((EX_DEV, total), jnp.float32),
+        in_specs=[pl.BlockSpec(memory_space=pl.ANY)] * 6,
+        out_specs=pl.BlockSpec(memory_space=pltpu.VMEM),
+        scratch_shapes=[
+            pltpu.VMEM(tokens_in.shape, jnp.bfloat16),
+            pltpu.VMEM(grad_out.shape, jnp.bfloat16),
+            pltpu.VMEM(proj_in.shape, jnp.bfloat16),
+            pltpu.VMEM(proj_out.shape, jnp.bfloat16),
+            pltpu.VMEM(segment_ids.shape, jnp.int32),
+            pltpu.VMEM((2 * rank, tok), jnp.float32),
+            pltpu.VMEM((rank + rank // 2, tok), jnp.float32),
+            pltpu.VMEM((total, cols), jnp.float32),
+            pltpu.VMEM((total, cols), jnp.float32),
+            pltpu.VMEM((total, 2 * total), jnp.float32),
+            pltpu.VMEM((total, 2 * total), jnp.float32),
+            dma((5,)),
+            dma((grad_out.shape[1] // CHUNK,)),
+            dma((2,)),
+            dma((2,)),
+            dma((n - 1,)),
+            dma((n - 1,)),
+            dma((n - 1,)),
+            dma((n - 1,)),
+            dma,
+            dma,
+        ],
+        compiler_params=pltpu.CompilerParams(
+            collective_id=0, has_side_effects=True, vmem_limit_bytes=50 * 2**20
+        ),
+    )(tokens_in, grad_out, proj_in, proj_out, segment_ids, query_grads)
 
 
 def solution(mesh):
@@ -76,8 +253,10 @@
 
     def per_device(*args):
         width = args[2].shape[1] ** 2
-        fewer = EX_DEV * mesh.shape["ex"] < width
-        return (dual if fewer else primal)(*args)
+        n = mesh.shape["ex"]
+        if EX_DEV * n == 128 and EX_DEV * n < width and mesh.shape["ffn"] == 2:
+            return dual(n, *args)
+        return primal(*args)
 
     return jax.shard_map(
         per_device, mesh=mesh, in_specs=in_specs, out_specs=out_specs, check_vma=False

time: 117 us -> 29.2 us (0.25)
  blocking collectives: 64.3 us -> 0 us
  Pallas kernels: 0 us -> 25.4 us
  other arithmetic: 24.1 us -> 0 us
  between operations: 14.1 us -> 0.04 us
  matrix products: 12.3 us -> 0 us
  local copies, waits for them, and re-layouts: 1.79 us -> 3.64 us
    all_gather x2 -> x0, blocking collectives: 64.3 us -> none  [the longest x1 33 us: dual(): queries = lax.all_gather(query_grads, 'ex', axis=0, tiled=True)]
    pallas_call x0 -> x1, Pallas kernels: none -> 25.4 us  [dual(): pl.pallas_call(functools.partial(kernel, n), out_shape=jax.ShapeDtypeStru...]
    another operation x6 -> x0, other arithmetic: 22.9 us -> none  [the longest x4 12.4 us: dual(): chol = jnp.linalg.cholesky(gram)]
    dot_general x6 -> x0, matrix products: 11.9 us -> none  [the longest x1 6.03 us: example_means(): out_part = jnp.dot(grad_out, proj_out, preferred_element_type=jnp.float32)]
    unnamed x8 -> x7, local copies, waits for them, and re-layouts: 1.6 us -> 3.64 us
  transfers between devices with their start and end apart: 1 -> 0, of which waited for: 0 -> 0; matrix products, arithmetic and copies ran while one was open for 0% -> 0% of each run, Pallas kernels for 0% -> 0%
where the time goes in v2:
time: 29.2 us; the launch traced here: 29.1 us
  Pallas kernels  25.4 us (87%)
  local copies, waits for them, and re-layouts  3.64 us (12%)
    pallas_call x1, Pallas kernels, dual(): pl.pallas_call(functools.partial(kernel, n), out_shape=jax.ShapeDtypeStru...  25.4 us
    unnamed x7, local copies, waits for them, and re-layouts  3.64 us

profile of v2, /device:TPU:0, one launch (start us, length us, event | category | flops | bytes accessed | tf_op | source)
XLA Modules:
  0.0 29.1 jit_solution(14884608630889615761)
XLA Ops:
  0.0 0.0 copy-start
  0.0 0.0 copy-start.1
  0.0 1.2 %copy.7.pin = bf16[2048,32]{1,0:T(8,128)(2,1)S(1)} copy(bf16[2048,32]{0,1:T(8,128)(2,1)} %param.8) | data formatting | bytes 262144 | tf_op args[2]
  1.2 1.8 %copy.8.pout = bf16[7168,32]{1,0:T(8,128)(2,1)S(1)} copy(bf16[7168,32]{0,1:T(8,128)(2,1)} %param.9) | data formatting | bytes 917504 | tf_op args[3]
  3.0 0.0 copy-done
  3.1 0.0 copy-done.1
  3.1 25.4 %shard_map.64 = f32[16,128]{1,0:T(8,128)S(1)} custom-call(bf16[512,2048]{1,0:T(8,128)(2,1)} %tok.1, bf16[512,7168]{1,0:T(8,128)(2,1)} %grad.1, bf16[2048,32]{1,0:T(8,128)(2,1)S(1)} %copy.7.pin, bf16[7168,32]{1,0:T(8,128)(2,1)S(1)} %copy.8.pout, s32[1,512]{1,0:T(1,128)S(1)} %copy-done.1, f32[16,1024]{1,0:T(8,128)S(1)} %copy-done), custom_call_target="tpu_custom_call" | custom-call | tf_op jit(solution)/shard_map/pallas_call | solution.py:209
  28.5 0.6 %copy.10 = f32[16,128]{1,0:T(8,128)} copy(f32[16,128]{1,0:T(8,128)S(1)} %shard_map.64) | data formatting | bytes 16384
Async XLA Ops:
  0.0 3.1 %copy-start = (f32[16,1024]{1,0:T(8,128)S(1)}, f32[16,1024]{1,0:T(8,128)}, u32[]{:S(2)}) copy-start(f32[16,1024]{1,0:T(8,128)} %qry.1) | copy-start | bytes 196612
  0.0 3.1 %copy-start.1 = (s32[1,512]{1,0:T(1,128)S(1)}, s32[1,512]{1,0:T(1,128)}, u32[]{:S(2)}) copy-start(s32[1,512]{1,0:T(1,128)} %seg.1) | copy-start | bytes 6148

commit v3 on v2

--- a/solution.py
+++ b/solution.py
@@ -65,7 +65,7 @@
     load_sem, chunk_sem, side_send, side_recv, e_send, e_recv, q_send, q_recv, p_send, p_recv,
 ):
     me, core = lax.axis_index("ex"), lax.axis_index("ffn")
-    rank = pin.shape[1]
+    rank = pin.shape[0]
     half = rank // 2
     width = rank * rank
     cols = width // 2
@@ -123,19 +123,21 @@
 
     loads[1].wait()
     loads[2].wait()
-    in_part = jnp.dot(tok_v[...], pin_v[...], preferred_element_type=jnp.float32)
-    mine[rank:, :] = in_part.T
+    in_part = lax.dot_general(pin_v[...], tok_v[...], NT, preferred_element_type=jnp.float32)
+    mine[rank:, :] = in_part
     in_copy = across(
         mine.at[pl.ds(rank, rank)], theirs.at[pl.ds(half, rank)], side_send.at[0], side_recv.at[0]
     )
 
     loads[3].wait()
-    acc = jnp.zeros((grad.shape[0], rank), jnp.float32)
+    acc = jnp.zeros((rank, grad.shape[0]), jnp.float32)
     for k, copy in enumerate(chunks):
         copy.wait()
         span = slice(k * CHUNK, (k + 1) * CHUNK)
-        acc += jnp.dot(grad_v[:, span], pout_v[span, :], preferred_element_type=jnp.float32)
-    mine[:rank, :] = acc.T
+        acc += lax.dot_general(
+            pout_v[:, span], grad_v[:, span], NT, preferred_element_type=jnp.float32
+        )
+    mine[:rank, :] = acc
     keep = pl.ds(pl.multiple_of(core * half, half), half)
     give = pl.ds(pl.multiple_of((1 - core) * half, half), half)
     out_copy = across(mine.at[give], theirs.at[pl.ds(0, half)], side_send.at[1], side_recv.at[1])
@@ -161,20 +163,19 @@
             block = jnp.where(place == k, sums[row : row + EX_DEV], block)
         e_all[rows, g * 128 : (g + 1) * 128] = block / counts
     e_copies = spread(e_all, e_send, e_recv)
+    for copy in e_copies:
+        copy.wait()
+
+    everyone = e_all[...]
+    part[:, :total] = dot_nt(everyone, everyone)
+    k_copy = across(part.at[:, :total], part_in.at[:, :total], p_send.at[0], p_recv.at[0])
     for copy in q_copies:
         copy.wait()
-    for copy in e_copies:
-        copy.wait()
-
-    everyone = e_all[...]
-    part[:, :total] = dot_nt(everyone, everyone)
     part[:, total:] = dot_nt(everyone, q_all[...])
-    p_copy = across(part, part_in, p_send, p_recv)
-    p_copy.wait()
-
-    whole = part[...] + part_in[...]
-    gram = whole[:, :total] * (1.0 / total)
-    cross = whole[:, total:]
+    g_copy = across(part.at[:, total:], part_in.at[:, total:], p_send.at[1], p_recv.at[1])
+    k_copy.wait()
+
+    gram = (part[:, :total] + part_in[:, :total]) * (1.0 / total)
     r = lax.broadcasted_iota(jnp.int32, (total, total), 0)
     c = lax.broadcasted_iota(jnp.int32, (total, total), 1)
     eye = (r == c).astype(jnp.float32)
@@ -198,6 +199,8 @@
     c16 = lax.broadcasted_iota(jnp.int32, (EX_DEV, total), 1)
     left = (r16 + me * EX_DEV == c16).astype(jnp.float32) - dot(own, gram)
     own = own + dot(left, x)
+    g_copy.wait()
+    cross = part[:, total:] + part_in[:, total:]
     out[...] = dot(own, cross) * (1.0 / width ** 0.5)
 
 
@@ -214,8 +217,8 @@
         scratch_shapes=[
             pltpu.VMEM(tokens_in.shape, jnp.bfloat16),
             pltpu.VMEM(grad_out.shape, jnp.bfloat16),
-            pltpu.VMEM(proj_in.shape, jnp.bfloat16),
-            pltpu.VMEM(proj_out.shape, jnp.bfloat16),
+            pltpu.VMEM(proj_in.shape[::-1], jnp.bfloat16),
+            pltpu.VMEM(proj_out.shape[::-1], jnp.bfloat16),
             pltpu.VMEM(segment_ids.shape, jnp.int32),
             pltpu.VMEM((2 * rank, tok), jnp.float32),
             pltpu.VMEM((rank + rank // 2, tok), jnp.float32),
@@ -231,13 +234,13 @@
             dma((n - 1,)),
             dma((n - 1,)),
             dma((n - 1,)),
-            dma,
-            dma,
+            dma((2,)),
+            dma((2,)),
         ],
         compiler_params=pltpu.CompilerParams(
-            collective_id=0, has_side_effects=True, vmem_limit_bytes=50 * 2**20
+            collective_id=0, has_side_effects=True, vmem_limit_bytes=60 * 2**20
         ),
-    )(tokens_in, grad_out, proj_in, proj_out, segment_ids, query_grads)
+    )(tokens_in, grad_out, proj_in.T, proj_out.T, segment_ids, query_grads)
 
 
 def solution(mesh):

time: 29.2 us -> 25.3 us (0.87)
  the two profiles are of different devices: /device:TPU:0 before, /device:TPU:13 now
where the time goes in v3:
time: 25.3 us; the launch traced here: 25.1 us
  Pallas kernels  23.8 us (94%)
  local copies, waits for them, and re-layouts  1.3 us (5%)
    pallas_call x1, Pallas kernels, dual(): pl.pallas_call(functools.partial(kernel, n), out_shape=jax.ShapeDtypeStru...  23.8 us
    unnamed x1, local copies, waits for them, and re-layouts  1.3 us

profile of v3, /device:TPU:13, one launch (start us, length us, event | category | flops | bytes accessed | tf_op | source)
XLA Modules:
  0.0 25.1 jit_solution(12909427362079725686)
XLA Ops:
  0.0 23.8 %shard_map.64 = f32[16,128]{1,0:T(8,128)} custom-call(bf16[512,2048]{1,0:T(8,128)(2,1)} %tok.1, bf16[512,7168]{1,0:T(8,128)(2,1)} %grad.1, bf16[32,2048]{1,0:T(8,128)(2,1)} %bitcast.3, bf16[32,7168]{1,0:T(8,128)(2,1)} %bitcast.2, s32[1,512]{1,0:T(1,128)} %seg.1, f32[16,1024]{1,0:T(8,128)} %qry.1), custom_call_target="tpu_custom_call" | custom-call | tf_op jit(solution)/shard_map/pallas_call | solution.py:212
  23.8 1.3 %copy.8 = f32[16,128]{1,0:T(8,128)} copy(f32[16,128]{1,0:T(8,128)} %shard_map.64) | data formatting | bytes 16384

commit v4 on v3

--- a/solution.py
+++ b/solution.py
@@ -211,7 +211,7 @@
     dma = pltpu.SemaphoreType.DMA
     return pl.pallas_call(
         functools.partial(kernel, n),
-        out_shape=jax.ShapeDtypeStruct((EX_DEV, total), jnp.float32),
+        out_shape=pltpu.VMEM((EX_DEV, total), jnp.float32),
         in_specs=[pl.BlockSpec(memory_space=pl.ANY)] * 6,
         out_specs=pl.BlockSpec(memory_space=pltpu.VMEM),
         scratch_shapes=[

time: 25.3 us -> 23.9 us (0.945)
  local copies, waits for them, and re-layouts: 1.3 us -> 0.6 us
  Pallas kernels: 23.8 us -> 23.2 us
    unnamed x1, local copies, waits for them, and re-layouts: 1.3 us -> 0.6 us
    pallas_call x1, Pallas kernels: 23.8 us -> 23.2 us  [dual(): pl.pallas_call(functools.partial(kernel, n), out_shape=pltpu.VMEM((EX_DEV...]
where the time goes in v4:
time: 23.9 us; the launch traced here: 23.8 us
  Pallas kernels  23.2 us (97%)
  local copies, waits for them, and re-layouts  0.6 us (3%)
    pallas_call x1, Pallas kernels, dual(): pl.pallas_call(functools.partial(kernel, n), out_shape=pltpu.VMEM((EX_DEV...  23.2 us
    unnamed x1, local copies, waits for them, and re-layouts  0.6 us

profile of v4, /device:TPU:13, one launch (start us, length us, event | category | flops | bytes accessed | tf_op | source)
XLA Modules:
  0.0 23.8 jit_solution(9963486587993912408)
XLA Ops:
  0.0 23.2 %shard_map.64 = f32[16,128]{1,0:T(8,128)S(1)} custom-call(bf16[512,2048]{1,0:T(8,128)(2,1)} %tok.1, bf16[512,7168]{1,0:T(8,128)(2,1)} %grad.1, bf16[32,2048]{1,0:T(8,128)(2,1)} %bitcast.3, bf16[32,7168]{1,0:T(8,128)(2,1)} %bitcast.2, s32[1,512]{1,0:T(1,128)} %seg.1, f32[16,1024]{1,0:T(8,128)} %qry.1), custom_call_target="tpu_custom_call" | custom-call | tf_op jit(solution)/shard_map/pallas_call | solution.py:212
  23.2 0.6 %copy.8 = f32[16,128]{1,0:T(8,128)} copy(f32[16,128]{1,0:T(8,128)S(1)} %shard_map.64) | data formatting | bytes 16384

commit v5 on v4

--- a/solution.py
+++ b/solution.py
@@ -46,8 +46,8 @@
     return jnp.dot(example_grads, gathered, precision=HIGH) / scale
 
 
-STEPS = 10
-CHUNK = 1024
+STEPS = 9
+CHUNK = 1792
 NT = (((1,), (1,)), ((), ()))
 
 
@@ -186,12 +186,16 @@
     bound = jnp.minimum(bound, trace + damping) * 1.0001
     low = damping / bound
     y = gram / bound
-    x = eye / bound
-    for _ in range(STEPS):
+    for step in range(STEPS):
         scale = 4.0 / ((1.0 + low) * (1.0 + low))
         factor = scale * ((1.0 + low) * eye - y)
-        both = dot(jnp.concatenate([y, x], axis=0), factor)
-        y, x = both[:total], both[total:]
+        if step == 0:
+            y, x = dot(y, factor), factor / bound
+        elif step == STEPS - 1:
+            x = dot(x, factor)
+        else:
+            both = dot(jnp.concatenate([y, x], axis=0), factor)
+            y, x = both[:total], both[total:]
         low = jnp.minimum(scale * low, 1.0)
     part_in[:, :total] = x
     own = part_in[rows, :total]

time: 23.9 us -> 22.6 us (0.946)
  the two profiles are of different devices: /device:TPU:13 before, /device:TPU:0 now
where the time goes in v5:
time: 22.6 us; the launch traced here: 22.3 us
  Pallas kernels  21.7 us (96%)
  local copies, waits for them, and re-layouts  0.6 us (3%)
    pallas_call x1, Pallas kernels, dual(): pl.pallas_call(functools.partial(kernel, n), out_shape=pltpu.VMEM((EX_DEV...  21.7 us
    unnamed x1, local copies, waits for them, and re-layouts  0.6 us

profile of v5, /device:TPU:0, one launch (start us, length us, event | category | flops | bytes accessed | tf_op | source)
XLA Modules:
  0.0 22.3 jit_solution(6404619577247468597)
XLA Ops:
  0.0 21.7 %shard_map.64 = f32[16,128]{1,0:T(8,128)S(1)} custom-call(bf16[512,2048]{1,0:T(8,128)(2,1)} %tok.1, bf16[512,7168]{1,0:T(8,128)(2,1)} %grad.1, bf16[32,2048]{1,0:T(8,128)(2,1)} %bitcast.3, bf16[32,7168]{1,0:T(8,128)(2,1)} %bitcast.2, s32[1,512]{1,0:T(1,128)} %seg.1, f32[16,1024]{1,0:T(8,128)} %qry.1), custom_call_target="tpu_custom_call" | custom-call | tf_op jit(solution)/shard_map/pallas_call | solution.py:216
  21.7 0.6 %copy.8 = f32[16,128]{1,0:T(8,128)} copy(f32[16,128]{1,0:T(8,128)S(1)} %shard_map.64) | data formatting | bytes 16384
